TPU v7x, 32 devices: a whole 2x2x4 slice. The times are simulated.
32 devices in a mesh: groups: 2 (over y), video: 8 (over z, x), fsdp: 2 (over core).
Axes of the slice: x: 2, y: 2, z: 4, core: 2. Of those that a mesh axis runs over, the one named last changes fastest.
Arguments:
- video: bfloat16 [32, 32, 16, 512], P(('groups', 'video', 'fsdp')), parts along dimension 0, may hold values from -6 to 6
- w_spatial: bfloat16 [3, 3, 512, 512], P(None, None, 'fsdp'), may hold values from -0.09375 to 0.09375
- norm_gain: float32 [512], replicated, may hold values from 0.1 to 1.9
- norm_shift: float32 [512], replicated, may hold values from -3 to 3
- w_time: bfloat16 [3, 512, 512], P(None, 'fsdp'), may hold values from -0.15625 to 0.15625
Outputs:
- result: bfloat16 [32, 32, 16, 512], P(('groups', 'video', 'fsdp')), parts along dimension 0
There are 2 independent parts, one for each index of `groups`. A program takes and returns all parts, laid end to end along the dimension named above; an argument that names none is the same for every part. Nothing has to cross between parts.
All inputs are finite; a program needn't handle non-finite values.
Results may differ from a plain program's by a relative error of at most 0.0049.
Values may be sent and summed in bfloat16 or wider, within the bound.
A program may use at most 64 MiB of HBM per device.

v0:
```python
import jax
import jax.numpy as jnp
from jax import lax
from jax.sharding import PartitionSpec as P

GROUPS = 32
CLIP = 16


def partner_2(block, axis, bit):
    count = lax.axis_size(axis)
    route = []
    for low in range(count):
        high = low | 1 << bit
        if high != low and high < count:
            route += [(low, high), (high, low)]
    return lax.ppermute(block, axis, route)


def spatial_conv(frames, w_spatial):
    count, height, width, channels = frames.shape
    outputs = w_spatial.shape[3]
    padded = jnp.pad(frames, ((0, 0), (1, 1), (1, 1), (0, 0)))
    initial = jnp.zeros((count * height * width, outputs), jnp.float32)
    total = initial
    piece = lax.all_gather(w_spatial, "fsdp", axis=2, tiled=True)
    span = piece.shape[2]
    for row_tap in range(3):
        for col_tap in range(3):
            window = padded[:, row_tap : row_tap + height, col_tap : col_tap + width, :].reshape(
                -1, span
            )
            total = total + jnp.dot(
                window, piece[row_tap, col_tap], preferred_element_type=jnp.float32
            )
    return total


def temporal_conv(stacked, w_time):
    rows = stacked[1].shape[0]
    outputs = w_time.shape[2]
    initial = jnp.zeros((rows, outputs), jnp.float32)
    total = initial
    piece = lax.all_gather(w_time, "fsdp", axis=1, tiled=True)
    for tap in range(3):
        columns = stacked[tap]
        total = total + jnp.dot(columns, piece[tap], preferred_element_type=jnp.float32)
    return total


def body(video, w_spatial, norm_gain, norm_shift, w_time):
    count, height, width, channels = video.shape
    spatial = spatial_conv(video, w_spatial)
    grouped = spatial.reshape(count, height * width, GROUPS, channels // GROUPS)
    mean = jnp.mean(grouped, axis=(1, 3), keepdims=True)
    variance = jnp.mean(jnp.square(grouped - mean), axis=(1, 3), keepdims=True)
    normed = ((grouped - mean) * lax.rsqrt(variance + 1e-05)).reshape(
        count, height * width, channels
    )
    hidden = jax.nn.silu(normed * norm_gain + norm_shift).astype(jnp.bfloat16)
    blocks = lax.axis_size("video")
    pairs = lax.axis_size("fsdp")
    pixels = height * width // blocks
    local = hidden.reshape(count, blocks, pixels, channels)
    arrived = lax.all_to_all(local, "video", split_axis=1, concat_axis=0, tiled=True)
    edges = jnp.stack([arrived[:, 0], arrived[:, count - 1]])
    partner = partner_2(edges, "fsdp", 0)
    other_first = partner[0]
    other_last = partner[1]
    side = lax.axis_index("fsdp")
    zero_block = jnp.zeros_like(other_last[:1])
    last_before = jnp.concatenate([zero_block, other_last[:-1]], axis=0)
    first_after = jnp.concatenate([other_first[1:], zero_block], axis=0)
    before_edge = jnp.where(side == 0, last_before, other_last)
    after_edge = jnp.where(side == 0, other_first, first_after)
    previous = jnp.concatenate([before_edge[:, None], arrived[:, :-1]], axis=1)
    following = jnp.concatenate([arrived[:, 1:], after_edge[:, None]], axis=1)
    frame_ids = (jnp.arange(blocks)[:, None] * pairs + side) * count + jnp.arange(count)[None, :]
    keep_before = (frame_ids % CLIP != 0)[:, :, None, None]
    keep_after = (frame_ids % CLIP != CLIP - 1)[:, :, None, None]
    previous = jnp.where(keep_before, previous, jnp.zeros_like(previous))
    following = jnp.where(keep_after, following, jnp.zeros_like(following))
    total = temporal_conv(
        (
            previous.reshape(-1, channels),
            arrived.reshape(-1, channels),
            following.reshape(-1, channels),
        ),
        w_time,
    )
    mixed = (arrived.reshape(-1, channels).astype(jnp.float32) + total).astype(jnp.bfloat16)
    mixed = mixed.reshape(blocks * count, 1, pixels, channels)
    returned = lax.all_to_all(mixed, "video", split_axis=0, concat_axis=1, tiled=True)
    return returned.reshape(count, height, width, channels)


def solution(mesh):
    placed = (
        P(("groups", "video", "fsdp"), None, None, None),
        P(None, None, "fsdp", None),
        P(),
        P(),
        P(None, "fsdp", None),
    )
    return jax.shard_map(
        body,
        mesh=mesh,
        in_specs=placed,
        out_specs=P(("groups", "video", "fsdp"), None, None, None),
        check_vma=False,
    )
```

profile of v0, /device:TPU:0, one launch (start us, length us, event | category | flops | bytes accessed | tf_op | source)
XLA Modules:
  0.0 88.9 jit_solution(9656500367549770682)
XLA Ops:
  6.5 0.0 all-gather.3.cloned.1.call-start
  6.5 0.7 all-gather.3.cloned.1.call-update
  7.3 5.2 %pad_slice_fusion = (bf16[1,32,16,512]{3,2,1,0:T(8,128)(2,1)S(1)}, bf16[1,32,16,512]{3,2,1,0:T(8,128)(2,1)}, bf16[1,32,16,512]{3,2,1,0:T(8,128)(2,1)S(1)}, bf16[...) fusion(bf16[1,32,16,512]{3,2,1,0:T(8,128)(2,1)} %param.5), kind=kLoop, calls=%fused_computation.12 | loop fusion | bytes 4718592 | tf_op jit(solution)/shard_map/slice | solution.py:30
  12.4 13.6 %all-gather.3.cloned.1.call-done = bf16[3,3,512,512]{3,2,1,0:T(8,128)(2,1)} async-done(((bf16[3,3,256,512]{3,2,1,0:T(8,128)(2,1)}), bf16[3,3,512,512]{3,2,1,0:T(8,128)(2,1)}) %all-gather.3.cloned.1.call-update) | async-done | bytes 4718608 | tf_op jit(solution)/shard_map/all_gather | solution.py:26
  26.1 0.0 copy-start
  26.1 1.8 %fusion.7 = f32[512,512]{1,0:T(8,128)S(1)} fusion(bf16[512,512]{1,0:T(8,128)(2,1)} %bitcast.101, bf16[3,3,512,512]{3,2,1,0:T(8,128)(2,1)} %all-gather.3.cloned.1.call-done), kind=kOutput, calls=%fused_computation.42 | convolution fusion | flops 268435456 | bytes 2097152 | tf_op jit(solution)/shard_map/dot_general | solution.py:33
  27.9 0.0 copy-start.1
  27.9 1.7 %convolution_add_fusion.9 = f32[512,512]{1,0:T(8,128)S(1)} fusion(f32[512,512]{1,0:T(8,128)S(1)} %fusion.7, bf16[512,512]{1,0:T(8,128)(2,1)} %bitcast.100, bf16[3,3,512,512]{3,2,1,0:T(8,128)(2,1)} %all-gather.3.cloned.1.call-done), kind=kOutput, calls=%fused_computation.10 | convolution fusion | flops 268697600 | bytes 3145728 | tf_op jit(solution)/shard_map/dot_general | solution.py:33
  29.6 0.0 copy-done
  29.6 0.4 convolution_add_fusion.8
  30.0 0.4 convolution_add_fusion.7
  30.5 0.0 copy-done.1
  30.5 0.4 convolution_add_fusion.6
  30.9 0.4 convolution_add_fusion.5
  31.4 0.0 copy-start.2
  31.4 0.0 copy-start.3
  31.4 0.4 convolution_add_fusion.4
  31.8 0.4 convolution_add_fusion.3
  32.3 0.5 fusion.9
  32.7 0.1 reduce_sum.24
  32.8 0.1 reduce_sum.25
  32.9 0.1 sub.21
  33.0 0.1 sub.22
  33.1 0.2 multiply_reduce_fusion
  33.3 0.1 reduce_sum.36
  33.4 0.1 reduce_sum.37
  33.5 0.1 mul.42
  33.6 0.1 mul.43
  33.6 0.0 copy-done.2
  33.7 0.0 copy-done.3
  33.7 1.1 %multiply_convert_fusion = bf16[512,512]{1,0:T(8,128)(2,1)} fusion(f32[512,512]{1,0:T(8,128)S(1)} %get-tuple-element.18, f32[512]{0:T(512)S(1)} %copy-done.2, f32[512]{0:T(512)S(1)} %copy-done.3, f32[512]{0:T(512)S(1)} %mul.43, f32[512]{0:T(512)S(1)} %sub.22), kind=kLoop, calls=%fused_computation.21 | loop fusion | flops 2359296 | bytes 1581056 | tf_op jit(solution)/shard_map/convert_element_type | solution.py:60
  34.8 5.8 %all-to-all-start = ((bf16[1,8,64,512]{3,2,0,1:T(8,128)(2,1)}), bf16[1,8,64,512]{3,2,0,1:T(8,128)(2,1)S(1)}, u32[]{:S(2)}, u32[]{:S(2)}) async-start(bf16[1,8,64,512]{3,2,0,1:T(8,128)(2,1)} %bitcast.19), calls=%async_computation | async-start | bytes 1048576 | tf_op jit(solution)/shard_map/all_to_all | solution.py:65
  40.6 0.0 all-gather.5.cloned.1.call-start
  40.6 0.7 all-gather.5.cloned.1.call-update
  41.3 14.2 %all-to-all-done = bf16[1,8,64,512]{3,2,0,1:T(8,128)(2,1)S(1)} async-done(((bf16[1,8,64,512]{3,2,0,1:T(8,128)(2,1)}), bf16[1,8,64,512]{3,2,0,1:T(8,128)(2,1)S(1)}, u32[]{:S(2)}, u32[]{:S(2)}) %all-to-all-start) | async-done | bytes 524320 | tf_op jit(solution)/shard_map/all_to_all | solution.py:65
  55.5 0.1 pad_maximum_fusion
  55.6 0.1 collective-permute-start
  55.7 2.6 %collective-permute-done = bf16[2,8,64,512]{3,2,0,1:T(8,128)(2,1)S(1)} collective-permute-done((bf16[2,8,64,512]{3,2,0,1:T(8,128)(2,1)S(1)}, bf16[2,8,64,512]{3,2,0,1:T(8,128)(2,1)S(1)}, u32[]{:S(2)}, u32[]{:S(2)}) %collective-permute-start) | collective-permute-done | bytes 1048608 | tf_op jit(solution)/shard_map/ppermute | solution.py:17
  58.3 0.1 slice_bitcast_fusion.26
  58.4 0.2 fusion.3
  58.6 0.0 all-gather.5.cloned.1.call-done
  58.6 1.5 %fusion.4 = f32[512,512]{1,0:T(8,128)S(1)} fusion(bf16[512,512]{1,0:T(8,128)(2,1)S(1)} %bitcast.105, bf16[3,512,512]{2,1,0:T(8,128)(2,1)} %all-gather.5.cloned.1.call-done), kind=kOutput, calls=%fused_computation.29 | convolution fusion | flops 268435456 | bytes 2097152 | tf_op jit(solution)/shard_map/dot_general | solution.py:47
  60.1 1.5 %convolution_add_fusion.1 = f32[512,512]{1,0:T(8,128)S(1)} fusion(f32[512,512]{1,0:T(8,128)S(1)} %fusion.4, bf16[512,512]{1,0:T(8,128)(2,1)S(1)} %bitcast.91, bf16[3,512,512]{2,1,0:T(8,128)(2,1)} %all-gather.5.cloned.1.call-done), kind=kOutput, calls=%fused_computation.2 | convolution fusion | flops 268697600 | bytes 3145728 | tf_op jit(solution)/shard_map/dot_general | solution.py:47
  61.6 1.5 %fusion.1 = bf16[512,512]{1,0:T(8,128)(2,1)S(1)} fusion(f32[512,512]{1,0:T(8,128)S(1)} %convolution_add_fusion.1, bf16[512,512]{1,0:T(8,128)(2,1)S(1)} %bitcast.104, bf16[512,512]{1,0:T(8,128)(2,1)S(1)} %bitcast.92, bf16[3,512,512]{2,1,0:T(8,128)(2,1)} %all-gather.5.cloned.1.call-done), kind=kOutput, calls=%fused_computation.11 | convolution fusion | flops 269484032 | bytes 3145728 | tf_op jit(solution)/shard_map/dot_general | solution.py:47
  63.1 18.2 %all_to_all.8 = bf16[8,1,64,512]{3,2,1,0:T(8,128)(2,1)S(1)} all-to-all(bf16[8,1,64,512]{3,2,1,0:T(8,128)(2,1)S(1)} %bitcast.103), channel_id=1, replica_groups=mesh['groups'=2,'video'=8,'fsdp'=2] {'video'}, dimensions={0} | all-to-all | bytes 1048576 | tf_op jit(solution)/shard_map/all_to_all | solution.py:93
  81.3 0.8 copy.15
  (3 shorter events, 0.0 us)
Async XLA Ops:
  6.5 19.5 %all-gather.3.cloned.1.call-start = ((), (), s32[]{:S(2)}) async-start(), calls=%async_computation.2 | async-start | bytes 7077888 | tf_op jit(solution)/shard_map/all_gather | solution.py:26
  26.1 3.5 %copy-start = (bf16[3,3,512,512]{3,2,1,0:T(8,128)(2,1)S(1)}, bf16[3,3,512,512]{3,2,1,0:T(8,128)(2,1)}, u32[]{:S(2)}) copy-start(bf16[3,3,512,512]{3,2,1,0:T(8,128)(2,1)} %all-gather.3.cloned.1.call-done) | copy-start | bytes 14155780
  27.9 2.6 %copy-start.1 = (bf16[1,32,16,512]{3,2,1,0:T(8,128)(2,1)S(1)}, bf16[1,32,16,512]{3,2,1,0:T(8,128)(2,1)}, u32[]{:S(2)}) copy-start(bf16[1,32,16,512]{3,2,1,0:T(8,128)(2,1)} %param.5) | copy-start | bytes 1572868
  31.4 2.3 %copy-start.2 = (f32[512]{0:T(512)S(1)}, f32[512]{0:T(512)}, u32[]{:S(2)}) copy-start(f32[512]{0:T(512)} %param.8) | copy-start | bytes 6148
  31.4 2.3 %copy-start.3 = (f32[512]{0:T(512)S(1)}, f32[512]{0:T(512)}, u32[]{:S(2)}) copy-start(f32[512]{0:T(512)} %param.7) | copy-start | bytes 6148
  34.8 20.7 %all-to-all-start = ((bf16[1,8,64,512]{3,2,0,1:T(8,128)(2,1)}), bf16[1,8,64,512]{3,2,0,1:T(8,128)(2,1)S(1)}, u32[]{:S(2)}, u32[]{:S(2)}) async-start(bf16[1,8,64,512]{3,2,0,1:T(8,128)(2,1)} %bitcast.19), calls=%async_computation | async-start | bytes 1048576 | tf_op jit(solution)/shard_map/all_to_all | solution.py:65
  40.6 18.0 %all-gather.5.cloned.1.call-start = ((), (), s32[]{:S(2)}) async-start(), calls=%async_computation.3 | async-start | bytes 2359296 | tf_op jit(solution)/shard_map/all_gather | solution.py:44
  55.6 2.7 %collective-permute-start = (bf16[2,8,64,512]{3,2,0,1:T(8,128)(2,1)S(1)}, bf16[2,8,64,512]{3,2,0,1:T(8,128)(2,1)S(1)}, u32[]{:S(2)}, u32[]{:S(2)}) collective-permute-start(bf16[2,8,64,512]{3,2,0,1:T(8,128)(2,1)S(1)} %pad_maximum_fusion), channel_id=1, source_target_pairs={{0,1},{1,0},{2,3},{3,2},{4,5},{5,4},{6,7},{7,6},{8,9},{9,8},{10,11... | collective-permute-start | bytes 3145736 | tf_op jit(solution)/shard_map/ppermute | solution.py:17
Sparse Core Ops, SparseCore 0:
  8.9 17.1 all-gather.2
  43.0 11.1 all-gather.4
where the time goes:
time: 89.3 us; the launch traced here: 88.9 us
  waiting for transfers between devices  31.9 us (36%)
  blocking collectives  18.2 us (20%)
  between operations  13.6 us (15%)
  matrix products  11 us (12%)
  local copies, waits for them, and re-layouts  6.52 us (7%)
  starting transfers between devices  5.88 us (7%)
  other arithmetic  1.84 us (2%)
    all_to_all x1, blocking collectives, body(): lax.all_to_all(mixed, 'video', split_axis=0, concat_axis=1, tiled=True)  18.2 us
    all_to_all x1, waiting for transfers between devices, body(): lax.all_to_all(local, 'video', split_axis=1, concat_axis=0, tiled=True)  14.2 us
    all_gather x1, waiting for transfers between devices, spatial_conv(): piece = lax.all_gather(w_spatial, 'fsdp', axis=2, tiled=True)  13.6 us
    dot_general x9, matrix products, spatial_conv(): jnp.dot(window, piece[row_tap, col_tap], preferred_element_type=jnp.float32)  6.53 us
    all_to_all x1, starting transfers between devices, body(): lax.all_to_all(local, 'video', split_axis=1, concat_axis=0, tiled=True)  5.77 us
    slice x1, local copies, waits for them, and re-layouts, spatial_conv(): padded[:, row_tap:row_tap + height, col_tap:col_tap + width, :]  5.18 us
    dot_general x3, matrix products, temporal_conv(): jnp.dot(columns, piece[tap], preferred_element_type=jnp.float32)  4.43 us
    ppermute x1, waiting for transfers between devices, partner_2(): return lax.ppermute(block, axis, route)  2.62 us
  transfers between devices with their start and end apart: 4, of which 3 were waited for; matrix products, arithmetic and copies ran while one was open for 6% of the time, Pallas kernels for 0%

commit v1 on v0

v1 whole, which is shorter than its diff:
```python
import functools

import jax
import jax.numpy as jnp
from jax import lax
from jax.experimental import pallas as pl
from jax.experimental.pallas import tpu as pltpu
from jax.sharding import PartitionSpec as P

GROUPS = 32
CLIP = 16
MESH = pl.DeviceIdType.MESH
CHUNK = 256


def kernel(
    width,
    group_size,
    video_ref,
    ws_ref,
    gain_ref,
    shift_ref,
    wt_ref,
    out_ref,
    raw,
    xs,
    ws,
    wt,
    acc,
    hid,
    near,
    far,
    local_sem,
    w_send,
    w_recv,
    near_send,
    near_recv,
    far_send,
    far_recv,
):
    rows = raw.shape[0]
    half = wt.shape[2]
    blocks = 2
    group = lax.axis_index("groups")
    block = lax.axis_index("video")
    side = lax.axis_index("fsdp")
    other = 1 - side
    position = (block * 2 + side) % CLIP
    has_far = position != side * (CLIP - 1)
    partner = (group, block, other)
    far_block = jnp.where(has_far, block + 2 * side - 1, block)
    distant = (group, far_block, other)

    video_copy = pltpu.make_async_copy(video_ref, raw, local_sem.at[0])
    ws_copy = pltpu.make_async_copy(ws_ref, ws.at[side], local_sem.at[1])
    wt_copy = pltpu.make_async_copy(wt_ref, wt.at[side], local_sem.at[2])
    video_copy.start()
    ws_copy.start()
    wt_copy.start()

    barrier = pltpu.get_barrier_semaphore()
    pl.semaphore_signal(barrier, inc=1, device_id=partner, device_id_type=MESH)

    @pl.when(has_far)
    def _():
        pl.semaphore_signal(barrier, inc=1, device_id=distant, device_id_type=MESH)

    pl.semaphore_wait(barrier, 1 + has_far.astype(jnp.int32))

    w_copies = []
    for nb in range(blocks):
        columns = pl.ds(nb * half, half)
        w_copies.append(
            pltpu.make_async_remote_copy(
                src_ref=ws_ref.at[:, :, columns],
                dst_ref=ws.at[side, :, :, columns],
                send_sem=w_send.at[nb],
                recv_sem=w_recv.at[nb],
                device_id=partner,
                device_id_type=MESH,
            )
        )
    w_copies.append(
        pltpu.make_async_remote_copy(
            src_ref=wt_ref,
            dst_ref=wt.at[side],
            send_sem=w_send.at[blocks],
            recv_sem=w_recv.at[blocks],
            device_id=partner,
            device_id_type=MESH,
        )
    )
    for copy in w_copies:
        copy.start()

    video_copy.wait()
    column = lax.broadcasted_iota(jnp.int32, (rows, half), 0) % width
    for h in range(blocks):
        centre = raw[:, h * half : (h + 1) * half]
        wide = centre.astype(jnp.float32)
        before = jnp.where(column != 0, pltpu.roll(wide, 1, 0), 0.0)
        after = jnp.where(column != width - 1, pltpu.roll(wide, rows - 1, 0), 0.0)
        edge = jnp.zeros((width, 3 * half), jnp.bfloat16)
        xs[h, 0:width, :] = edge
        xs[h, width + rows : 2 * width + rows, :] = edge
        xs[h, width : width + rows, 0:half] = before.astype(jnp.bfloat16)
        xs[h, width : width + rows, half : 2 * half] = centre
        xs[h, width : width + rows, 2 * half : 3 * half] = after.astype(jnp.bfloat16)

    def conv(h, nb, first):
        def step(m, carry):
            start = pl.multiple_of(m * CHUNK, CHUNK)
            total = None
            for dy in range(3):
                part = jnp.dot(
                    xs[h, pl.ds(start + dy * width, CHUNK), :],
                    ws[h, dy, :, nb * half : (nb + 1) * half],
                    preferred_element_type=jnp.float32,
                )
                total = part if total is None else total + part
            if not first:
                total = total + acc[nb, pl.ds(start, CHUNK), :]
            acc[nb, pl.ds(start, CHUNK), :] = total
            return carry

        lax.fori_loop(0, rows // CHUNK, step, 0)

    ws_copy.wait()
    for nb in range(blocks):
        conv(side, nb, True)

    same = (
        lax.broadcasted_iota(jnp.int32, (half, half), 0) // group_size
        == lax.broadcasted_iota(jnp.int32, (half, half), 1) // group_size
    ).astype(jnp.float32)

    def spread(sums):
        wide = jnp.broadcast_to(sums, (8, half))
        total = jnp.dot(
            wide, same, preferred_element_type=jnp.float32, precision=lax.Precision.HIGHEST
        )
        return total[0:1] / (rows * group_size)

    h_copies = []
    for nb in range(blocks):
        w_copies[nb].wait_recv()
        conv(other, nb, False)
        mean = spread(jnp.sum(acc[nb], axis=0, keepdims=True))
        variance = spread(jnp.sum(jnp.square(acc[nb] - mean), axis=0, keepdims=True))
        span = slice(nb * half, (nb + 1) * half)
        scale = lax.rsqrt(variance + 1e-05) * gain_ref[:, span]
        v = (acc[nb] - mean) * scale + shift_ref[:, span]
        hid[nb] = (v / (1.0 + jnp.exp(-v))).astype(jnp.bfloat16)
        near_copy = pltpu.make_async_remote_copy(
            src_ref=hid.at[nb],
            dst_ref=near.at[nb],
            send_sem=near_send.at[nb],
            recv_sem=near_recv.at[nb],
            device_id=partner,
            device_id_type=MESH,
        )
        far_copy = pltpu.make_async_remote_copy(
            src_ref=hid.at[nb],
            dst_ref=far.at[nb],
            send_sem=far_send.at[nb],
            recv_sem=far_recv.at[nb],
            device_id=distant,
            device_id_type=MESH,
        )

        @pl.when(has_far)
        def _():
            far_copy.start()

        near_copy.start()
        h_copies.append((near_copy, far_copy))

    def mix(frame, tap, nb):
        def step(m, carry):
            spot = pl.ds(pl.multiple_of(m * CHUNK, CHUNK), CHUNK)
            for ob in range(blocks):
                part = jnp.dot(
                    frame[nb, spot, :],
                    wt[nb, tap, :, ob * half : (ob + 1) * half],
                    preferred_element_type=jnp.float32,
                )
                acc[ob, spot, :] = acc[ob, spot, :] + part
            return carry

        lax.fori_loop(0, rows // CHUNK, step, 0)

    wt_copy.wait()
    w_copies[blocks].wait_recv()
    for nb in range(blocks):
        acc[nb] = hid[nb].astype(jnp.float32)
    for nb in range(blocks):
        mix(hid, 1, nb)
    for nb in range(blocks):
        h_copies[nb][0].wait_recv()
        mix(near, 2 * other, nb)

    @pl.when(has_far)
    def _():
        for nb in range(blocks):
            h_copies[nb][1].wait_recv()
            mix(far, 2 * side, nb)

    for nb in range(blocks):
        out_ref[:, nb * half : (nb + 1) * half] = acc[nb].astype(jnp.bfloat16)

    for copy in w_copies:
        copy.wait_send()
    for nb in range(blocks):
        h_copies[nb][0].wait_send()

    @pl.when(has_far)
    def _():
        for nb in range(blocks):
            h_copies[nb][1].wait_send()


def body(video, w_spatial, norm_gain, norm_shift, w_time):
    count, height, width, channels = video.shape
    half = w_time.shape[1]
    assert count == 1 and 2 * half == channels
    rows = height * width
    bf16 = jnp.bfloat16
    vmem = pl.BlockSpec(memory_space=pltpu.VMEM)
    hbm = pl.BlockSpec(memory_space=pl.ANY)
    dma = pltpu.SemaphoreType.DMA
    out = pl.pallas_call(
        functools.partial(kernel, width, channels // GROUPS),
        out_shape=jax.ShapeDtypeStruct((rows, channels), bf16),
        in_specs=[hbm, hbm, vmem, vmem, hbm],
        out_specs=vmem,
        scratch_shapes=[
            pltpu.VMEM((rows, channels), bf16),
            pltpu.VMEM((2, rows + 2 * width, 3 * half), bf16),
            pltpu.VMEM((2, 3, 3 * half, channels), bf16),
            pltpu.VMEM((2, 3, half, channels), bf16),
            pltpu.VMEM((2, rows, half), jnp.float32),
            pltpu.VMEM((2, rows, half), bf16),
            pltpu.VMEM((2, rows, half), bf16),
            pltpu.VMEM((2, rows, half), bf16),
            dma((3,)),
            dma((3,)),
            dma((3,)),
            dma((2,)),
            dma((2,)),
            dma((2,)),
            dma((2,)),
        ],
        compiler_params=pltpu.CompilerParams(
            collective_id=0, has_side_effects=True, vmem_limit_bytes=48 * 1024 * 1024
        ),
    )(
        video.reshape(rows, channels),
        w_spatial.reshape(3, 3 * half, channels),
        norm_gain.reshape(1, channels),
        norm_shift.reshape(1, channels),
        w_time,
    )
    return out.reshape(video.shape)


def solution(mesh):
    placed = (
        P(("groups", "video", "fsdp"), None, None, None),
        P(None, None, "fsdp", None),
        P(),
        P(),
        P(None, "fsdp", None),
    )
    return jax.shard_map(
        body,
        mesh=mesh,
        in_specs=placed,
        out_specs=P(("groups", "video", "fsdp"), None, None, None),
        check_vma=False,
    )
```

time: 89.3 us -> 26.5 us (0.30)
  the two profiles are of different devices: /device:TPU:0 before, /device:TPU:13 now
where the time goes in v1:
time: 26.5 us; the launch traced here: 26.2 us
  Pallas kernels  20.2 us (76%)
  local copies, waits for them, and re-layouts  6 us (23%)
    pallas_call x1, Pallas kernels, body(): pl.pallas_call(functools.partial(kernel, width, channels // GROUPS), out_...  20.2 us
    unnamed x11, local copies, waits for them, and re-layouts  6 us

profile of v1, /device:TPU:13, one launch (start us, length us, event | category | flops | bytes accessed | tf_op | source)
XLA Modules:
  0.0 26.2 jit_solution(17834654842957623780)
XLA Ops:
  0.0 0.0 copy-start
  0.0 1.7 %copy-done = bf16[3,3,256,512]{3,2,1,0:T(8,128)(2,1)S(1)} copy-done((bf16[3,3,256,512]{3,2,1,0:T(8,128)(2,1)S(1)}, bf16[3,3,256,512]{3,2,1,0:T(8,128)(2,1)}, u32[]{:S(2)}) %copy-start) | copy-done | bytes 2359320
  1.7 0.0 copy-start.1
  1.7 1.1 %copy-done.1 = bf16[3,256,512]{2,1,0:T(8,128)(2,1)S(1)} copy-done((bf16[3,256,512]{2,1,0:T(8,128)(2,1)S(1)}, bf16[3,256,512]{2,1,0:T(8,128)(2,1)}, u32[]{:S(2)}) %copy-start.1) | copy-done | bytes 786456
  2.8 0.0 copy-start.2
  2.8 1.0 %copy-done.2 = bf16[1,32,16,512]{3,2,1,0:T(8,128)(2,1)S(1)} copy-done((bf16[1,32,16,512]{3,2,1,0:T(8,128)(2,1)S(1)}, bf16[1,32,16,512]{3,2,1,0:T(8,128)(2,1)}, u32[]{:S(2)}) %copy-start.2) | copy-done | bytes 524312
  3.8 0.0 copy-start.3
  3.8 0.7 %copy-done.3 = f32[512]{0:T(512)S(1)} copy-done((f32[512]{0:T(512)S(1)}, f32[512]{0:T(512)}, u32[]{:S(2)}) %copy-start.3) | copy-done | bytes 2072
  4.5 0.0 copy-start.4
  4.5 0.7 %copy-done.4 = f32[512]{0:T(512)S(1)} copy-done((f32[512]{0:T(512)S(1)}, f32[512]{0:T(512)}, u32[]{:S(2)}) %copy-start.4) | copy-done | bytes 2072
  5.2 20.2 %shard_map.55 = bf16[512,512]{1,0:T(8,128)(2,1)S(1)} custom-call(bf16[512,512]{1,0:T(8,128)(2,1)S(1)} %bitcast.7, bf16[3,768,512]{2,1,0:T(8,128)(2,1)S(1)} %bitcast.5, f32[1,512]{1,0:T(1,128)S(1)} %bitcast.8, f32[1,512]{1,0:T(1,128)S(1)} %bitcast.9, bf16[3,256,512]{2,1,0:T(8,128)(2,1)S(1)} %copy-done.1), custom_call_target="tpu_custom_call" | custom-call | tf_op jit(solution)/shard_map/pallas_call | solution.py:231
  25.4 0.8 %copy.7 = bf16[1,32,16,512]{3,2,1,0:T(8,128)(2,1)} copy(bf16[1,32,16,512]{3,2,1,0:T(8,128)(2,1)S(1)} %bitcast.6) | data formatting | bytes 1048576
Async XLA Ops:
  0.0 1.7 %copy-start = (bf16[3,3,256,512]{3,2,1,0:T(8,128)(2,1)S(1)}, bf16[3,3,256,512]{3,2,1,0:T(8,128)(2,1)}, u32[]{:S(2)}) copy-start(bf16[3,3,256,512]{3,2,1,0:T(8,128)(2,1)} %param.6) | copy-start | bytes 7077892
  1.7 1.1 %copy-start.1 = (bf16[3,256,512]{2,1,0:T(8,128)(2,1)S(1)}, bf16[3,256,512]{2,1,0:T(8,128)(2,1)}, u32[]{:S(2)}) copy-start(bf16[3,256,512]{2,1,0:T(8,128)(2,1)} %wt_ref.1) | copy-start | bytes 2359300
  2.8 1.0 %copy-start.2 = (bf16[1,32,16,512]{3,2,1,0:T(8,128)(2,1)S(1)}, bf16[1,32,16,512]{3,2,1,0:T(8,128)(2,1)}, u32[]{:S(2)}) copy-start(bf16[1,32,16,512]{3,2,1,0:T(8,128)(2,1)} %param.5) | copy-start | bytes 1572868
  3.8 0.7 %copy-start.3 = (f32[512]{0:T(512)S(1)}, f32[512]{0:T(512)}, u32[]{:S(2)}) copy-start(f32[512]{0:T(512)} %param.7) | copy-start | bytes 6148
  4.5 0.7 %copy-start.4 = (f32[512]{0:T(512)S(1)}, f32[512]{0:T(512)}, u32[]{:S(2)}) copy-start(f32[512]{0:T(512)} %param.8) | copy-start | bytes 6148

commit v2 on v1

--- a/solution.py
+++ b/solution.py
@@ -11,6 +11,7 @@
 CLIP = 16
 MESH = pl.DeviceIdType.MESH
 CHUNK = 256
+PARTS = 4
 
 
 def kernel(
@@ -18,8 +19,8 @@
     group_size,
     video_ref,
     ws_ref,
-    gain_ref,
-    shift_ref,
+    gain_hbm,
+    shift_hbm,
     wt_ref,
     out_ref,
     raw,
@@ -29,7 +30,12 @@
     acc,
     hid,
     near,
-    far,
+    gain_ref,
+    shift_ref,
+    far_raw,
+    far_xs,
+    stats,
+    far_stats,
     local_sem,
     w_send,
     w_recv,
@@ -37,6 +43,8 @@
     near_recv,
     far_send,
     far_recv,
+    stat_send,
+    stat_recv,
 ):
     rows = raw.shape[0]
     half = wt.shape[2]
@@ -54,9 +62,13 @@
     video_copy = pltpu.make_async_copy(video_ref, raw, local_sem.at[0])
     ws_copy = pltpu.make_async_copy(ws_ref, ws.at[side], local_sem.at[1])
     wt_copy = pltpu.make_async_copy(wt_ref, wt.at[side], local_sem.at[2])
+    gain_copy = pltpu.make_async_copy(gain_hbm, gain_ref, local_sem.at[3])
+    shift_copy = pltpu.make_async_copy(shift_hbm, shift_ref, local_sem.at[4])
     video_copy.start()
     ws_copy.start()
     wt_copy.start()
+    gain_copy.start()
+    shift_copy.start()
 
     barrier = pltpu.get_barrier_semaphore()
     pl.semaphore_signal(barrier, inc=1, device_id=partner, device_id_type=MESH)
@@ -66,6 +78,27 @@
         pl.semaphore_signal(barrier, inc=1, device_id=distant, device_id_type=MESH)
 
     pl.semaphore_wait(barrier, 1 + has_far.astype(jnp.int32))
+
+    step_rows = rows // PARTS
+    bounds = [0] + [step_rows * p + width for p in range(1, PARTS)] + [rows]
+    far_copies = []
+    for p in range(PARTS):
+        span = pl.ds(bounds[p], bounds[p + 1] - bounds[p])
+        far_copies.append(
+            pltpu.make_async_remote_copy(
+                src_ref=video_ref.at[span],
+                dst_ref=far_raw.at[span],
+                send_sem=far_send.at[p],
+                recv_sem=far_recv.at[p],
+                device_id=distant,
+                device_id_type=MESH,
+            )
+        )
+
+    @pl.when(has_far)
+    def _():
+        for copy in far_copies:
+            copy.start()
 
     w_copies = []
     for nb in range(blocks):
@@ -94,18 +127,29 @@
         copy.start()
 
     video_copy.wait()
-    column = lax.broadcasted_iota(jnp.int32, (rows, half), 0) % width
-    for h in range(blocks):
-        centre = raw[:, h * half : (h + 1) * half]
-        wide = centre.astype(jnp.float32)
-        before = jnp.where(column != 0, pltpu.roll(wide, 1, 0), 0.0)
-        after = jnp.where(column != width - 1, pltpu.roll(wide, rows - 1, 0), 0.0)
+
+    def taps(source, target, low, high):
+        count = high - low
+        column = lax.broadcasted_iota(jnp.int32, (count, half), 0) % width
+        for h in range(blocks):
+            centre = source[low:high, h * half : (h + 1) * half]
+            wide = centre.astype(jnp.float32)
+            before = jnp.where(column != 0, pltpu.roll(wide, 1, 0), 0.0)
+            after = jnp.where(column != width - 1, pltpu.roll(wide, count - 1, 0), 0.0)
+            here = slice(width + low, width + high)
+            target[h, here, 0:half] = before.astype(jnp.bfloat16)
+            target[h, here, half : 2 * half] = centre
+            target[h, here, 2 * half : 3 * half] = after.astype(jnp.bfloat16)
+
+    def edges(target):
         edge = jnp.zeros((width, 3 * half), jnp.bfloat16)
-        xs[h, 0:width, :] = edge
-        xs[h, width + rows : 2 * width + rows, :] = edge
-        xs[h, width : width + rows, 0:half] = before.astype(jnp.bfloat16)
-        xs[h, width : width + rows, half : 2 * half] = centre
-        xs[h, width : width + rows, 2 * half : 3 * half] = after.astype(jnp.bfloat16)
+        for h in range(blocks):
+            target[h, 0:width, :] = edge
+            target[h, width + rows : 2 * width + rows, :] = edge
+
+    edges(xs)
+    edges(far_xs)
+    taps(raw, xs, 0, rows)
 
     def conv(h, nb, first):
         def step(m, carry):
@@ -141,6 +185,16 @@
         )
         return total[0:1] / (rows * group_size)
 
+    stat_copy = pltpu.make_async_remote_copy(
+        src_ref=stats,
+        dst_ref=far_stats,
+        send_sem=stat_send.at[0],
+        recv_sem=stat_recv.at[0],
+        device_id=distant,
+        device_id_type=MESH,
+    )
+    gain_copy.wait()
+    shift_copy.wait()
     h_copies = []
     for nb in range(blocks):
         w_copies[nb].wait_recv()
@@ -159,21 +213,14 @@
             device_id=partner,
             device_id_type=MESH,
         )
-        far_copy = pltpu.make_async_remote_copy(
-            src_ref=hid.at[nb],
-            dst_ref=far.at[nb],
-            send_sem=far_send.at[nb],
-            recv_sem=far_recv.at[nb],
-            device_id=distant,
-            device_id_type=MESH,
-        )
-
-        @pl.when(has_far)
-        def _():
-            far_copy.start()
-
         near_copy.start()
-        h_copies.append((near_copy, far_copy))
+        h_copies.append(near_copy)
+        stats[nb, 0] = jnp.broadcast_to(mean, (8, half))
+        stats[nb, 1] = jnp.broadcast_to(scale, (8, half))
+
+    @pl.when(has_far)
+    def _():
+        stat_copy.start()
 
     def mix(frame, tap, nb):
         def step(m, carry):
@@ -195,28 +242,54 @@
         acc[nb] = hid[nb].astype(jnp.float32)
     for nb in range(blocks):
         mix(hid, 1, nb)
-    for nb in range(blocks):
-        h_copies[nb][0].wait_recv()
+
+    def far_part(p):
+        far_copies[p].wait_recv()
+        taps(far_raw, far_xs, bounds[p], bounds[p + 1])
+        low = p * step_rows
+        here = slice(low, low + step_rows)
+        if p == 0:
+            stat_copy.wait_recv()
+        for nb in range(blocks):
+            total = None
+            for h in range(blocks):
+                for dy in range(3):
+                    part = jnp.dot(
+                        far_xs[h, low + dy * width : low + dy * width + step_rows, :],
+                        ws[h, dy, :, nb * half : (nb + 1) * half],
+                        preferred_element_type=jnp.float32,
+                    )
+                    total = part if total is None else total + part
+            v = (total - far_stats[nb, 0, 0:1]) * far_stats[nb, 1, 0:1]
+            v = v + shift_ref[:, nb * half : (nb + 1) * half]
+            frame = (v / (1.0 + jnp.exp(-v))).astype(jnp.bfloat16)
+            for ob in range(blocks):
+                acc[ob, here, :] = acc[ob, here, :] + jnp.dot(
+                    frame,
+                    wt[nb, 2 * side, :, ob * half : (ob + 1) * half],
+                    preferred_element_type=jnp.float32,
+                )
+
+    for nb in range(blocks):
+        h_copies[nb].wait_recv()
         mix(near, 2 * other, nb)
 
     @pl.when(has_far)
     def _():
-        for nb in range(blocks):
-            h_copies[nb][1].wait_recv()
-            mix(far, 2 * side, nb)
+        for p in range(PARTS):
+            far_part(p)
 
     for nb in range(blocks):
         out_ref[:, nb * half : (nb + 1) * half] = acc[nb].astype(jnp.bfloat16)
 
-    for copy in w_copies:
+    for copy in w_copies + h_copies:
         copy.wait_send()
-    for nb in range(blocks):
-        h_copies[nb][0].wait_send()
-
-    @pl.when(has_far)
-    def _():
-        for nb in range(blocks):
-            h_copies[nb][1].wait_send()
+
+    @pl.when(has_far)
+    def _():
+        for copy in far_copies:
+            copy.wait_send()
+        stat_copy.wait_send()
 
 
 def body(video, w_spatial, norm_gain, norm_shift, w_time):
@@ -226,12 +299,12 @@
     rows = height * width
     bf16 = jnp.bfloat16
     vmem = pl.BlockSpec(memory_space=pltpu.VMEM)
-    hbm = pl.BlockSpec(memory_space=pl.ANY)
+    hbm = pl.BlockSpec(memory_space=pltpu.HBM)
     dma = pltpu.SemaphoreType.DMA
     out = pl.pallas_call(
         functools.partial(kernel, width, channels // GROUPS),
         out_shape=jax.ShapeDtypeStruct((rows, channels), bf16),
-        in_specs=[hbm, hbm, vmem, vmem, hbm],
+        in_specs=[hbm] * 5,
         out_specs=vmem,
         scratch_shapes=[
             pltpu.VMEM((rows, channels), bf16),
@@ -241,17 +314,24 @@
             pltpu.VMEM((2, rows, half), jnp.float32),
             pltpu.VMEM((2, rows, half), bf16),
             pltpu.VMEM((2, rows, half), bf16),
-            pltpu.VMEM((2, rows, half), bf16),
-            dma((3,)),
+            pltpu.VMEM((1, channels), jnp.float32),
+            pltpu.VMEM((1, channels), jnp.float32),
+            pltpu.VMEM((rows, channels), bf16),
+            pltpu.VMEM((2, rows + 2 * width, 3 * half), bf16),
+            pltpu.VMEM((2, 2, 8, half), jnp.float32),
+            pltpu.VMEM((2, 2, 8, half), jnp.float32),
+            dma((5,)),
             dma((3,)),
             dma((3,)),
             dma((2,)),
             dma((2,)),
-            dma((2,)),
-            dma((2,)),
+            dma((PARTS,)),
+            dma((PARTS,)),
+            dma((1,)),
+            dma((1,)),
         ],
         compiler_params=pltpu.CompilerParams(
-            collective_id=0, has_side_effects=True, vmem_limit_bytes=48 * 1024 * 1024
+            collective_id=0, has_side_effects=True, vmem_limit_bytes=63 * 1024 * 1024
         ),
     )(
         video.reshape(rows, channels),

time: 26.5 us -> 24.8 us (0.936)
  local copies, waits for them, and re-layouts: 6 us -> 1.87 us
  Pallas kernels: 20.2 us -> 22.8 us
    unnamed x11 -> x1, local copies, waits for them, and re-layouts: 6 us -> 1.87 us
    pallas_call x1, Pallas kernels: 20.2 us -> 22.8 us  [body(): pl.pallas_call(functools.partial(kernel, width, channels // GROUPS), out_...]
where the time goes in v2:
time: 24.8 us; the launch traced here: 24.7 us
  Pallas kernels  22.8 us (92%)
  local copies, waits for them, and re-layouts  1.87 us (8%)
    pallas_call x1, Pallas kernels, body(): pl.pallas_call(functools.partial(kernel, width, channels // GROUPS), out_...  22.8 us
    unnamed x1, local copies, waits for them, and re-layouts  1.87 us

profile of v2, /device:TPU:13, one launch (start us, length us, event | category | flops | bytes accessed | tf_op | source)
XLA Modules:
  0.0 24.7 jit_solution(7971875894511308117)
XLA Ops:
  0.0 22.8 %shard_map.55 = bf16[512,512]{1,0:T(8,128)(2,1)} custom-call(bf16[512,512]{1,0:T(8,128)(2,1)} %bitcast.7, bf16[3,768,512]{2,1,0:T(8,128)(2,1)} %bitcast.5, f32[1,512]{1,0:T(1,128)} %bitcast.8, f32[1,512]{1,0:T(1,128)} %bitcast.9, bf16[3,256,512]{2,1,0:T(8,128)(2,1)} %wt_ref.1), custom_call_target="tpu_custom_call" | custom-call | tf_op jit(solution)/shard_map/pallas_call | solution.py:304
  22.8 1.9 %copy.7 = bf16[1,32,16,512]{3,2,1,0:T(8,128)(2,1)} copy(bf16[1,32,16,512]{3,2,1,0:T(8,128)(2,1)} %bitcast.6) | data formatting | bytes 1048576

commit v3 on v2

--- a/solution.py
+++ b/solution.py
@@ -11,7 +11,7 @@
 CLIP = 16
 MESH = pl.DeviceIdType.MESH
 CHUNK = 256
-PARTS = 4
+PARTS = 1
 
 
 def kernel(
@@ -36,6 +36,7 @@
     far_xs,
     stats,
     far_stats,
+    far_hid,
     local_sem,
     w_send,
     w_recv,
@@ -45,6 +46,8 @@
     far_recv,
     stat_send,
     stat_recv,
+    late_send,
+    late_recv,
 ):
     rows = raw.shape[0]
     half = wt.shape[2]
@@ -79,8 +82,9 @@
 
     pl.semaphore_wait(barrier, 1 + has_far.astype(jnp.int32))
 
-    step_rows = rows // PARTS
-    bounds = [0] + [step_rows * p + width for p in range(1, PARTS)] + [rows]
+    early = rows // 2
+    step_rows = early // PARTS
+    bounds = [0] + [step_rows * (p + 1) + width for p in range(PARTS)]
     far_copies = []
     for p in range(PARTS):
         span = pl.ds(bounds[p], bounds[p + 1] - bounds[p])
@@ -105,8 +109,8 @@
         columns = pl.ds(nb * half, half)
         w_copies.append(
             pltpu.make_async_remote_copy(
-                src_ref=ws_ref.at[:, :, columns],
-                dst_ref=ws.at[side, :, :, columns],
+                src_ref=ws_ref.at[:, columns],
+                dst_ref=ws.at[side, :, columns],
                 send_sem=w_send.at[nb],
                 recv_sem=w_recv.at[nb],
                 device_id=partner,
@@ -148,20 +152,23 @@
             target[h, width + rows : 2 * width + rows, :] = edge
 
     edges(xs)
-    edges(far_xs)
+    for h in range(blocks):
+        far_xs[h, 0:width, :] = jnp.zeros((width, 3 * half), jnp.bfloat16)
     taps(raw, xs, 0, rows)
+
+    def windows(source, h, start, count):
+        return jnp.concatenate(
+            [source[h, pl.ds(start + dy * width, count), :] for dy in range(3)], axis=1
+        )
 
     def conv(h, nb, first):
         def step(m, carry):
             start = pl.multiple_of(m * CHUNK, CHUNK)
-            total = None
-            for dy in range(3):
-                part = jnp.dot(
-                    xs[h, pl.ds(start + dy * width, CHUNK), :],
-                    ws[h, dy, :, nb * half : (nb + 1) * half],
-                    preferred_element_type=jnp.float32,
-                )
-                total = part if total is None else total + part
+            total = jnp.dot(
+                windows(xs, h, start, CHUNK),
+                ws[h, :, nb * half : (nb + 1) * half],
+                preferred_element_type=jnp.float32,
+            )
             if not first:
                 total = total + acc[nb, pl.ds(start, CHUNK), :]
             acc[nb, pl.ds(start, CHUNK), :] = total
@@ -185,14 +192,28 @@
         )
         return total[0:1] / (rows * group_size)
 
-    stat_copy = pltpu.make_async_remote_copy(
-        src_ref=stats,
-        dst_ref=far_stats,
-        send_sem=stat_send.at[0],
-        recv_sem=stat_recv.at[0],
-        device_id=distant,
-        device_id_type=MESH,
-    )
+    stat_copies, late_copies = [], []
+    for nb in range(blocks):
+        stat_copies.append(
+            pltpu.make_async_remote_copy(
+                src_ref=stats.at[nb],
+                dst_ref=far_stats.at[nb],
+                send_sem=stat_send.at[nb],
+                recv_sem=stat_recv.at[nb],
+                device_id=distant,
+                device_id_type=MESH,
+            )
+        )
+        late_copies.append(
+            pltpu.make_async_remote_copy(
+                src_ref=hid.at[nb, pl.ds(early, rows - early)],
+                dst_ref=far_hid.at[nb],
+                send_sem=late_send.at[nb],
+                recv_sem=late_recv.at[nb],
+                device_id=distant,
+                device_id_type=MESH,
+            )
+        )
     gain_copy.wait()
     shift_copy.wait()
     h_copies = []
@@ -203,8 +224,20 @@
         variance = spread(jnp.sum(jnp.square(acc[nb] - mean), axis=0, keepdims=True))
         span = slice(nb * half, (nb + 1) * half)
         scale = lax.rsqrt(variance + 1e-05) * gain_ref[:, span]
+        stats[nb, 0] = jnp.broadcast_to(mean, (8, half))
+        stats[nb, 1] = jnp.broadcast_to(scale, (8, half))
+
+        @pl.when(has_far)
+        def _():
+            stat_copies[nb].start()
+
         v = (acc[nb] - mean) * scale + shift_ref[:, span]
         hid[nb] = (v / (1.0 + jnp.exp(-v))).astype(jnp.bfloat16)
+
+        @pl.when(has_far)
+        def _():
+            late_copies[nb].start()
+
         near_copy = pltpu.make_async_remote_copy(
             src_ref=hid.at[nb],
             dst_ref=near.at[nb],
@@ -215,12 +248,6 @@
         )
         near_copy.start()
         h_copies.append(near_copy)
-        stats[nb, 0] = jnp.broadcast_to(mean, (8, half))
-        stats[nb, 1] = jnp.broadcast_to(scale, (8, half))
-
-    @pl.when(has_far)
-    def _():
-        stat_copy.start()
 
     def mix(frame, tap, nb):
         def step(m, carry):
@@ -248,18 +275,18 @@
         taps(far_raw, far_xs, bounds[p], bounds[p + 1])
         low = p * step_rows
         here = slice(low, low + step_rows)
-        if p == 0:
-            stat_copy.wait_recv()
         for nb in range(blocks):
-            total = None
-            for h in range(blocks):
-                for dy in range(3):
-                    part = jnp.dot(
-                        far_xs[h, low + dy * width : low + dy * width + step_rows, :],
-                        ws[h, dy, :, nb * half : (nb + 1) * half],
-                        preferred_element_type=jnp.float32,
-                    )
-                    total = part if total is None else total + part
+            if p == 0:
+                stat_copies[nb].wait_recv()
+            total = jnp.dot(
+                windows(far_xs, 0, low, step_rows),
+                ws[0, :, nb * half : (nb + 1) * half],
+                preferred_element_type=jnp.float32,
+            ) + jnp.dot(
+                windows(far_xs, 1, low, step_rows),
+                ws[1, :, nb * half : (nb + 1) * half],
+                preferred_element_type=jnp.float32,
+            )
             v = (total - far_stats[nb, 0, 0:1]) * far_stats[nb, 1, 0:1]
             v = v + shift_ref[:, nb * half : (nb + 1) * half]
             frame = (v / (1.0 + jnp.exp(-v))).astype(jnp.bfloat16)
@@ -278,6 +305,14 @@
     def _():
         for p in range(PARTS):
             far_part(p)
+        for nb in range(blocks):
+            late_copies[nb].wait_recv()
+            for ob in range(blocks):
+                acc[ob, early:rows, :] = acc[ob, early:rows, :] + jnp.dot(
+                    far_hid[nb],
+                    wt[nb, 2 * side, :, ob * half : (ob + 1) * half],
+                    preferred_element_type=jnp.float32,
+                )
 
     for nb in range(blocks):
         out_ref[:, nb * half : (nb + 1) * half] = acc[nb].astype(jnp.bfloat16)
@@ -287,9 +322,8 @@
 
     @pl.when(has_far)
     def _():
-        for copy in far_copies:
+        for copy in far_copies + stat_copies + late_copies:
             copy.wait_send()
-        stat_copy.wait_send()
 
 
 def body(video, w_spatial, norm_gain, norm_shift, w_time):
@@ -309,17 +343,18 @@
         scratch_shapes=[
             pltpu.VMEM((rows, channels), bf16),
             pltpu.VMEM((2, rows + 2 * width, 3 * half), bf16),
-            pltpu.VMEM((2, 3, 3 * half, channels), bf16),
+            pltpu.VMEM((2, 9 * half, channels), bf16),
             pltpu.VMEM((2, 3, half, channels), bf16),
             pltpu.VMEM((2, rows, half), jnp.float32),
             pltpu.VMEM((2, rows, half), bf16),
             pltpu.VMEM((2, rows, half), bf16),
             pltpu.VMEM((1, channels), jnp.float32),
             pltpu.VMEM((1, channels), jnp.float32),
-            pltpu.VMEM((rows, channels), bf16),
-            pltpu.VMEM((2, rows + 2 * width, 3 * half), bf16),
+            pltpu.VMEM((rows // 2 + width, channels), bf16),
+            pltpu.VMEM((2, rows // 2 + 2 * width, 3 * half), bf16),
             pltpu.VMEM((2, 2, 8, half), jnp.float32),
             pltpu.VMEM((2, 2, 8, half), jnp.float32),
+            pltpu.VMEM((2, rows - rows // 2, half), bf16),
             dma((5,)),
             dma((3,)),
             dma((3,)),
@@ -327,15 +362,17 @@
             dma((2,)),
             dma((PARTS,)),
             dma((PARTS,)),
-            dma((1,)),
-            dma((1,)),
+            dma((2,)),
+            dma((2,)),
+            dma((2,)),
+            dma((2,)),
         ],
         compiler_params=pltpu.CompilerParams(
             collective_id=0, has_side_effects=True, vmem_limit_bytes=63 * 1024 * 1024
         ),
     )(
         video.reshape(rows, channels),
-        w_spatial.reshape(3, 3 * half, channels),
+        w_spatial.reshape(9 * half, channels),
         norm_gain.reshape(1, channels),
         norm_shift.reshape(1, channels),
         w_time,

time: 24.8 us -> 19.3 us (0.78)
  Pallas kernels: 22.8 us -> 17.3 us
    pallas_call x1, Pallas kernels: 22.8 us -> 17.3 us  [body(): pl.pallas_call(functools.partial(kernel, width, channels // GROUPS), out_...]
where the time goes in v3:
time: 19.3 us; the launch traced here: 19.2 us
  Pallas kernels  17.3 us (90%)
  local copies, waits for them, and re-layouts  1.87 us (10%)
    pallas_call x1, Pallas kernels, body(): pl.pallas_call(functools.partial(kernel, width, channels // GROUPS), out_...  17.3 us
    unnamed x1, local copies, waits for them, and re-layouts  1.87 us

profile of v3, /device:TPU:13, one launch (start us, length us, event | category | flops | bytes accessed | tf_op | source)
XLA Modules:
  0.0 19.2 jit_solution(14210622136993319949)
XLA Ops:
  0.0 17.3 %shard_map.55 = bf16[512,512]{1,0:T(8,128)(2,1)} custom-call(bf16[512,512]{1,0:T(8,128)(2,1)} %bitcast.7, bf16[2304,512]{1,0:T(8,128)(2,1)} %bitcast.5, f32[1,512]{1,0:T(1,128)} %bitcast.8, f32[1,512]{1,0:T(1,128)} %bitcast.9, bf16[3,256,512]{2,1,0:T(8,128)(2,1)} %wt_ref.1), custom_call_target="tpu_custom_call" | custom-call | tf_op jit(solution)/shard_map/pallas_call | solution.py:338
  17.3 1.9 %copy.7 = bf16[1,32,16,512]{3,2,1,0:T(8,128)(2,1)} copy(bf16[1,32,16,512]{3,2,1,0:T(8,128)(2,1)} %bitcast.6) | data formatting | bytes 1048576

commit v4 on v3

--- a/solution.py
+++ b/solution.py
@@ -368,14 +368,19 @@
             dma((2,)),
         ],
         compiler_params=pltpu.CompilerParams(
-            collective_id=0, has_side_effects=True, vmem_limit_bytes=63 * 1024 * 1024
+            collective_id=0, has_side_effects=True, vmem_limit_bytes=48 * 1024 * 1024
         ),
     )(
-        video.reshape(rows, channels),
-        w_spatial.reshape(9 * half, channels),
-        norm_gain.reshape(1, channels),
-        norm_shift.reshape(1, channels),
-        w_time,
+        *[
+            pltpu.with_memory_space_constraint(array, pltpu.HBM)
+            for array in (
+                video.reshape(rows, channels),
+                w_spatial.reshape(9 * half, channels),
+                norm_gain.reshape(1, channels),
+                norm_shift.reshape(1, channels),
+                w_time,
+            )
+        ]
     )
     return out.reshape(video.shape)
 

time: 19.3 us -> 17.5 us (0.907)
  local copies, waits for them, and re-layouts: 1.87 us -> 0.8 us
  Pallas kernels: 17.3 us -> 16.5 us
    unnamed x1, local copies, waits for them, and re-layouts: 1.87 us -> 0.8 us
    pallas_call x1, Pallas kernels: 17.3 us -> 16.5 us  [body(): pl.pallas_call(functools.partial(kernel, width, channels // GROUPS), out_...]
where the time goes in v4:
time: 17.5 us; the launch traced here: 17.3 us
  Pallas kernels  16.5 us (94%)
  local copies, waits for them, and re-layouts  0.8 us (5%)
    pallas_call x1, Pallas kernels, body(): pl.pallas_call(functools.partial(kernel, width, channels // GROUPS), out_...  16.5 us
    unnamed x1, local copies, waits for them, and re-layouts  0.8 us

profile of v4, /device:TPU:13, one launch (start us, length us, event | category | flops | bytes accessed | tf_op | source)
XLA Modules:
  0.0 17.3 jit_solution(8138403088834696319)
XLA Ops:
  0.0 16.5 %shard_map.55 = bf16[512,512]{1,0:T(8,128)(2,1)S(1)} custom-call(bf16[512,512]{1,0:T(8,128)(2,1)} %bitcast.7, bf16[2304,512]{1,0:T(8,128)(2,1)} %bitcast.6, f32[1,512]{1,0:T(1,128)} %bitcast.8, f32[1,512]{1,0:T(1,128)} %bitcast.9, bf16[3,256,512]{2,1,0:T(8,128)(2,1)} %wt_ref.1), custom_call_target="tpu_custom_call" | custom-call | tf_op jit(solution)/shard_map/pallas_call | solution.py:338
  16.5 0.8 %copy.7 = bf16[1,32,16,512]{3,2,1,0:T(8,128)(2,1)} copy(bf16[1,32,16,512]{3,2,1,0:T(8,128)(2,1)S(1)} %bitcast.5) | data formatting | bytes 1048576

commit v5 on v4

--- a/solution.py
+++ b/solution.py
@@ -305,6 +305,16 @@
     def _():
         for p in range(PARTS):
             far_part(p)
+
+    def emit(low, high):
+        for nb in range(blocks):
+            part = acc[nb, low:high, :].astype(jnp.bfloat16)
+            out_ref[low:high, nb * half : (nb + 1) * half] = part
+
+    emit(0, early)
+
+    @pl.when(has_far)
+    def _():
         for nb in range(blocks):
             late_copies[nb].wait_recv()
             for ob in range(blocks):
@@ -314,8 +324,7 @@
                     preferred_element_type=jnp.float32,
                 )
 
-    for nb in range(blocks):
-        out_ref[:, nb * half : (nb + 1) * half] = acc[nb].astype(jnp.bfloat16)
+    emit(early, rows)
 
     for copy in w_copies + h_copies:
         copy.wait_send()

time: 17.5 us -> 17.4 us (level)
  no operation moved by 1% of the time
where the time goes in v5:
time: 17.4 us; the launch traced here: 17.2 us
  Pallas kernels  16.4 us (94%)
  local copies, waits for them, and re-layouts  0.8 us (5%)
    pallas_call x1, Pallas kernels, body(): pl.pallas_call(functools.partial(kernel, width, channels // GROUPS), out_...  16.4 us
    unnamed x1, local copies, waits for them, and re-layouts  0.8 us

profile of v5, /device:TPU:13, one launch (start us, length us, event | category | flops | bytes accessed | tf_op | source)
XLA Modules:
  0.0 17.2 jit_solution(13712828607141669083)
XLA Ops:
  0.0 16.4 %shard_map.55 = bf16[512,512]{1,0:T(8,128)(2,1)S(1)} custom-call(bf16[512,512]{1,0:T(8,128)(2,1)} %bitcast.7, bf16[2304,512]{1,0:T(8,128)(2,1)} %bitcast.6, f32[1,512]{1,0:T(1,128)} %bitcast.8, f32[1,512]{1,0:T(1,128)} %bitcast.9, bf16[3,256,512]{2,1,0:T(8,128)(2,1)} %wt_ref.1), custom_call_target="tpu_custom_call" | custom-call | tf_op jit(solution)/shard_map/pallas_call | solution.py:347
  16.4 0.8 %copy.7 = bf16[1,32,16,512]{3,2,1,0:T(8,128)(2,1)} copy(bf16[1,32,16,512]{3,2,1,0:T(8,128)(2,1)S(1)} %bitcast.5) | data formatting | bytes 1048576

commit v6 on v5

--- a/solution.py
+++ b/solution.py
@@ -82,7 +82,7 @@
 
     pl.semaphore_wait(barrier, 1 + has_far.astype(jnp.int32))
 
-    early = rows // 2
+    early = rows * 5 // 8
     step_rows = early // PARTS
     bounds = [0] + [step_rows * (p + 1) + width for p in range(PARTS)]
     far_copies = []
@@ -359,11 +359,11 @@
             pltpu.VMEM((2, rows, half), bf16),
             pltpu.VMEM((1, channels), jnp.float32),
             pltpu.VMEM((1, channels), jnp.float32),
-            pltpu.VMEM((rows // 2 + width, channels), bf16),
-            pltpu.VMEM((2, rows // 2 + 2 * width, 3 * half), bf16),
+            pltpu.VMEM((rows * 5 // 8 + width, channels), bf16),
+            pltpu.VMEM((2, rows * 5 // 8 + 2 * width, 3 * half), bf16),
             pltpu.VMEM((2, 2, 8, half), jnp.float32),
             pltpu.VMEM((2, 2, 8, half), jnp.float32),
-            pltpu.VMEM((2, rows - rows // 2, half), bf16),
+            pltpu.VMEM((2, rows - rows * 5 // 8, half), bf16),
             dma((5,)),
             dma((3,)),
             dma((3,)),

time: 17.4 us -> 18.7 us (1.075)
  Pallas kernels: 16.4 us -> 17.8 us
    pallas_call x1, Pallas kernels: 16.4 us -> 17.8 us  [body(): pl.pallas_call(functools.partial(kernel, width, channels // GROUPS), out_...]
where the time goes in v6:
time: 18.7 us; the launch traced here: 18.6 us
  Pallas kernels  17.8 us (95%)
  local copies, waits for them, and re-layouts  0.8 us (4%)
    pallas_call x1, Pallas kernels, body(): pl.pallas_call(functools.partial(kernel, width, channels // GROUPS), out_...  17.8 us
    unnamed x1, local copies, waits for them, and re-layouts  0.8 us

profile of v6, /device:TPU:13, one launch (start us, length us, event | category | flops | bytes accessed | tf_op | source)
XLA Modules:
  0.0 18.6 jit_solution(10461197138980957488)
XLA Ops:
  0.0 17.8 %shard_map.55 = bf16[512,512]{1,0:T(8,128)(2,1)S(1)} custom-call(bf16[512,512]{1,0:T(8,128)(2,1)} %bitcast.7, bf16[2304,512]{1,0:T(8,128)(2,1)} %bitcast.6, f32[1,512]{1,0:T(1,128)} %bitcast.8, f32[1,512]{1,0:T(1,128)} %bitcast.9, bf16[3,256,512]{2,1,0:T(8,128)(2,1)} %wt_ref.1), custom_call_target="tpu_custom_call" | custom-call | tf_op jit(solution)/shard_map/pallas_call | solution.py:347
  17.8 0.8 %copy.7 = bf16[1,32,16,512]{3,2,1,0:T(8,128)(2,1)} copy(bf16[1,32,16,512]{3,2,1,0:T(8,128)(2,1)S(1)} %bitcast.5) | data formatting | bytes 1048576
